TPU v7x, 512 devices: a whole 4x8x8 slice. The times are simulated.
512 devices in a mesh: row: 16 (over y, core), col: 32 (over x, z).
Axes of the slice: x: 4, y: 8, z: 8, core: 2. Of those that a mesh axis runs over, the one named last changes fastest.
Arguments:
- panel_rhs: bfloat16 [2, 2048, 1024], P(None, 'row'), may hold values from -6 to 6
- diag_inverse: bfloat16 [2, 2048, 2048], P(None, 'col', 'row'), may hold values from -0.125 to 0.125
- cross_block: bfloat16 [2048, 2048], P('row', 'col'), may hold values from -0.125 to 0.125
- trail_factor: bfloat16 [16384, 2, 2048], P('row', None, 'col'), may hold values from -0.09375 to 0.09375
- trail_rhs: float32 [16384, 1024], P('row', 'col'), may hold values from -6 to 6
Outputs:
- solved: bfloat16 [2, 2048, 1024], P(None, 'col')
- trail_new: float32 [16384, 1024], P('row', 'col')
All inputs are finite; a program needn't handle non-finite values.
Results may differ from a plain program's by a relative error of at most 0.015.
Values may be sent and summed in bfloat16 or wider, within the bound.
A program may use at most 64 MiB of HBM per device.

v0:
```python
import jax
import jax.numpy as jnp
from jax import lax
from jax.sharding import PartitionSpec as P


def panel_solve(inverse, right_side):
    partial_rows = jnp.dot(inverse, right_side, preferred_element_type=jnp.float32)
    return lax.psum(partial_rows, "row").astype(jnp.bfloat16)


def per_device(panel_rhs, diag_inverse, cross_block, trail_factor, trail_rhs):
    first_panel = panel_solve(diag_inverse[0], panel_rhs[0])
    crossed = lax.psum(jnp.dot(cross_block, first_panel, preferred_element_type=jnp.float32), "col")
    reduced = (panel_rhs[1].astype(jnp.float32) - crossed).astype(jnp.bfloat16)
    second_panel = panel_solve(diag_inverse[1], reduced)
    solved = jnp.stack([first_panel, second_panel])
    trail_count = trail_factor.shape[0]
    flat_factor = trail_factor.reshape(trail_count, -1)
    update = jnp.dot(
        flat_factor, solved.reshape(-1, solved.shape[2]), preferred_element_type=jnp.float32
    )
    update_share = lax.psum_scatter(
        update.astype(jnp.bfloat16), "col", scatter_dimension=1, tiled=True
    ).astype(jnp.float32)
    return (solved, trail_rhs - update_share)


def solution(mesh):
    in_specs = (
        P(None, "row", None),
        P(None, "col", "row"),
        P("row", "col"),
        P("row", None, "col"),
        P("row", "col"),
    )
    out_specs = (P(None, "col", None), P("row", "col"))
    return jax.shard_map(
        per_device, mesh=mesh, in_specs=in_specs, out_specs=out_specs, check_vma=False
    )
```

profile of v0, /device:TPU:1, one launch (start us, length us, event | category | flops | bytes accessed | tf_op | source)
XLA Modules:
  0.0 496.4 jit_solution(13017692040946824796)
XLA Ops:
  7.2 0.0 copy-start
  7.2 0.0 copy-start.4
  7.2 0.0 copy-start.2
  7.2 0.0 all-reduce.4.cloned.1.call-start
  7.2 1.2 fusion.4
  8.5 51.2 %all-reduce.5 = bf16[64,1024]{1,0:T(8,128)(2,1)S(1)} all-reduce(f32[64,1024]{1,0:T(8,128)S(1)} %fusion.4), channel_id=1, replica_groups=mesh['row'=16,'col'=32] {'row'}, use_global_device_ids=true, to_apply=%region_0.0 | all-reduce | flops 65536 | bytes 393216 | tf_op jit(solution)/shard_map/psum | solution.py:9
  59.7 1.8 convolution_bitcast_fusion
  61.5 0.0 all-reduce.4.cloned.1.call-update
  61.5 0.0 reduce-scatter.2.cloned.1.call-start
  61.6 156.9 %all-reduce.4.cloned.1.call-done = f32[128,1024]{1,0:T(8,128)} async-done(((f32[128,1024]{1,0:T(8,128)}), f32[128,1024]{1,0:T(8,128)}) %all-reduce.4.cloned.1.call-update) | async-done | bytes 524304 | tf_op jit(solution)/shard_map/psum | solution.py:14
  218.5 0.0 copy-done.4
  218.5 0.0 copy-done.2
  218.5 1.2 convolution_bitcast_fusion.1
  219.7 49.5 %all-reduce.6 = bf16[64,1024]{1,0:T(8,128)(2,1)S(1)} all-reduce(f32[64,1024]{1,0:T(8,128)S(1)} %convolution_bitcast_fusion.1), channel_id=1, replica_groups=mesh['row'=16,'col'=32] {'row'}, use_global_device_ids=true, to_apply=%region_2.0 | all-reduce | flops 65536 | bytes 393216 | tf_op jit(solution)/shard_map/psum | solution.py:9
  269.3 0.0 copy-done
  269.3 0.0 copy-start.1
  269.3 0.0 copy-start.3
  269.3 2.1 fusion
  271.4 0.0 reduce-scatter.2.cloned.1.call-update
  271.4 0.0 copy-done.1
  271.4 216.6 %reduce-scatter.2.cloned.1.call-done = bf16[1024,32]{0,1:T(8,128)(2,1)} async-done(((bf16[1024,1024]{0,1:T(8,128)(2,1)}), bf16[1024,32]{0,1:T(8,128)(2,1)}) %reduce-scatter.2.cloned.1.call-update) | async-done | bytes 65552 | tf_op jit(solution)/shard_map/reduce_scatter | solution.py:23
  488.0 0.0 copy-done.3
  488.1 1.5 convert_subtract_fusion.1
  (1 shorter events, 0.0 us)
Async XLA Ops:
  7.2 262.1 %copy-start = (bf16[1024,2,64]{0,2,1:T(8,128)(2,1)S(1)}, bf16[1024,2,64]{0,2,1:T(8,128)(2,1)}, u32[]{:S(2)}) copy-start(bf16[1024,2,64]{0,2,1:T(8,128)(2,1)} %param.8) | copy-start | bytes 786436
  7.2 211.3 %copy-start.4 = (bf16[2,64,128]{2,1,0:T(8,128)(2,1)S(1)}, bf16[2,64,128]{2,1,0:T(8,128)(2,1)}, u32[]{:S(2)}) copy-start(bf16[2,64,128]{2,1,0:T(8,128)(2,1)} %param.6) | copy-start | bytes 98308
  7.2 211.3 %copy-start.2 = (bf16[2,128,1024]{2,1,0:T(8,128)(2,1)S(1)}, bf16[2,128,1024]{2,1,0:T(8,128)(2,1)}, u32[]{:S(2)}) copy-start(bf16[2,128,1024]{2,1,0:T(8,128)(2,1)} %param.5) | copy-start | bytes 1572868
  7.2 211.3 %all-reduce.4.cloned.1.call-start = ((), (), s32[]{:S(2)}) async-start(), calls=%async_computation.1 | async-start | bytes 1048576 | tf_op jit(solution)/shard_map/psum | solution.py:14
  61.5 426.5 %reduce-scatter.2.cloned.1.call-start = ((), (), s32[]{:S(2)}) async-start(), calls=%async_computation.2 | async-start | bytes 2162688 | tf_op jit(solution)/shard_map/reduce_scatter | solution.py:23
  269.3 2.1 copy-start.1
  269.3 218.8 %copy-start.3 = (f32[1024,32]{0,1:T(8,128)S(1)}, f32[1024,32]{0,1:T(8,128)}, u32[]{:S(2)}) copy-start(f32[1024,32]{0,1:T(8,128)} %param.9) | copy-start | bytes 393220
Sparse Core Ops, SparseCore 0:
  61.6 156.7 all-reduce.3
  271.5 216.4 reduce-scatter.1
where the time goes:
time: 501 us; the launch traced here: 496 us
  waiting for transfers between devices  374 us (75%)
  blocking collectives  101 us (20%)
  between operations  14.1 us (3%)
  matrix products  6.33 us (1%)
    reduce_scatter x1, waiting for transfers between devices, per_device(): lax.psum_scatter(update.astype(jnp.bfloat16), 'col', scatter_dimension=1,...  217 us
    psum x1, waiting for transfers between devices, per_device(): lax.psum(jnp.dot(cross_block, first_panel, preferred_element_type=jnp.flo...  157 us
    psum x2, blocking collectives, panel_solve(): return lax.psum(partial_rows, 'row').astype(jnp.bfloat16)  101 us
  transfers between devices with their start and end apart: 2, of which 2 were waited for; matrix products, arithmetic and copies ran while one was open for 0% of the time, Pallas kernels for 0%

commit v1 on v0

v1 whole, which is shorter than its diff:
```python
import functools

import jax
import jax.numpy as jnp
from jax import lax
from jax.experimental import pallas as pl
from jax.experimental.pallas import tpu as pltpu
from jax.sharding import PartitionSpec as P

MESH = pl.DeviceIdType.MESH
BF16 = jnp.bfloat16
F32 = jnp.float32


def contract_rows(left, right):
    return lax.dot_general(left, right, (((0,), (0,)), ((), ())), preferred_element_type=F32)


def contract(left, right):
    return jnp.dot(left, right, preferred_element_type=F32)


def kernel(
    R, X, Z,
    rhs, diag, cross, trail, old,
    solved, new,
    trail_all, diag_all, cross_all, partial, sent, landed, panels, cross_sent, cross_landed,
    update, update_sent, update_landed, rows_landed, spread,
    local_sem, near_send, near_recv, trail_send, trail_recv, sum_send, sum_recv,
    rows_send, rows_recv, last_send, last_recv,
):
    row, col = lax.axis_index("row"), lax.axis_index("col")
    x, z = col // Z, lax.rem(col, Z)
    bc, br = diag.shape[1:]
    nrhs = rhs.shape[2]
    share = nrhs // (X * Z)
    width = share * X
    piece = Z * bc // R

    def row_peer(d):
        return lax.rem(row + d, R)

    def x_peer(d):
        return lax.rem(x + d, X)

    def z_peer(d):
        return lax.rem(z + d + Z, Z)

    def send(src, dst, send_sem, recv_sem, where):
        copy = pltpu.make_async_remote_copy(
            src_ref=src, dst_ref=dst, send_sem=send_sem, recv_sem=recv_sem,
            device_id=where, device_id_type=MESH,
        )
        copy.start()

    def drain(ref, sem):
        pltpu.make_async_copy(ref, ref, sem).wait()

    trail_own = pltpu.make_async_copy(trail, trail_all.at[:, z], local_sem.at[0])
    trail_own.start()

    barrier = pltpu.get_barrier_semaphore()
    for d in range(1, R):
        pl.semaphore_signal(barrier, inc=1, device_id=(row_peer(d), col), device_id_type=MESH)
    for d in range(1, X):
        pl.semaphore_signal(barrier, inc=1, device_id=(row, x_peer(d) * Z + z), device_id_type=MESH)
    for d in range(1, Z):
        pl.semaphore_signal(barrier, inc=1, device_id=(row, x * Z + z_peer(d)), device_id_type=MESH)

    diag_all[0, z] = diag[0]
    diag_all[1, z] = diag[1]
    cross_all[z] = cross[...]
    source = lax.broadcasted_iota(jnp.int32, (nrhs, width), 0)
    lane = lax.broadcasted_iota(jnp.int32, (nrhs, width), 1)
    pick = (source == ((lane // share) * Z + z) * share + lane % share).astype(F32).astype(BF16)
    rhs_first = contract(rhs[0], pick).astype(BF16)
    rhs_second = contract(rhs[1], pick)
    trail_own.wait()

    pl.semaphore_wait(barrier, (R - 1) + (X - 1) + (Z - 1))

    order = sorted(range(1, Z), key=lambda d: -min(d, Z - d))
    for d in order:
        send(diag_all.at[0, z], diag_all.at[0, z], near_send.at[0], near_recv.at[0], (row, x * Z + z_peer(d)))
    for d in order:
        send(cross_all.at[z], cross_all.at[z], near_send.at[1], near_recv.at[1], (row, x * Z + z_peer(d)))
    for d in order:
        send(diag_all.at[1, z], diag_all.at[1, z], near_send.at[2], near_recv.at[2], (row, x * Z + z_peer(d)))

    half = Z // 2

    def ring_has(way, panel, step):
        return step < half or (step == half and way == panel)

    def ring_send(step):
        for panel in range(2):
            for way in range(2):
                if ring_has(way, panel, step):
                    sign = 1 - 2 * way
                    block = z_peer(-sign * (step - 1))
                    send(
                        trail_all.at[panel, block], trail_all.at[panel, block],
                        trail_send.at[way, panel, step - 1], trail_recv.at[way, panel, step - 1],
                        (row, x * Z + z_peer(sign)),
                    )

    def ring_wait(step, panels_in=(0, 1)):
        for panel in panels_in:
            for way in range(2):
                if ring_has(way, panel, step):
                    drain(trail_all.at[panel, 0], trail_recv.at[way, panel, step - 1])

    def ring_drain():
        for step in range(1, half + 1):
            for panel in range(2):
                for way in range(2):
                    if ring_has(way, panel, step):
                        drain(trail_all.at[panel, 0], trail_send.at[way, panel, step - 1])

    ring_send(1)

    def scatter(panel, right_side):
        total = contract(diag_all[panel].reshape(Z * bc, br), right_side)
        partial[...] = total
        sent[panel] = total.astype(BF16).reshape(R, piece, width)
        for d in range(1, R):
            send(sent.at[panel, row_peer(d)], landed.at[panel, d - 1], sum_send.at[panel, 0],
                 sum_recv.at[panel, 0], (row_peer(d), col))

    def gather(panel):
        drain(landed.at[panel], sum_recv.at[panel, 0])
        mine = pl.ds(pl.multiple_of(row * piece, piece), piece)
        total = partial[mine, :]
        for d in range(R - 1):
            total = total + landed[panel, d].astype(F32)
        panels[panel, mine, :] = total.astype(BF16)
        for d in range(1, R):
            send(panels.at[panel, mine, :], panels.at[panel, mine, :], sum_send.at[panel, 1],
                 sum_recv.at[panel, 1], (row_peer(d), col))

    def gathered(panel):
        drain(panels.at[panel, pl.ds(0, (R - 1) * piece), :], sum_recv.at[panel, 1])

    def spread_rows(panel):
        own = panels[panel, pl.ds(pl.multiple_of(z * bc, bc), bc), :]
        rows_landed[panel, z] = own
        for d in order:
            theirs = pl.ds(pl.multiple_of(z_peer(d) * bc, bc), bc)
            send(panels.at[panel, theirs, :], rows_landed.at[panel, z], rows_send.at[panel],
                 rows_recv.at[panel], (row, x * Z + z_peer(d)))

    def write_rows(panel):
        drain(rows_landed.at[panel, pl.ds(0, Z - 1)], rows_recv.at[panel])
        total = contract(rows_landed[panel, 0], spread[0])
        for block in range(1, Z):
            total = total + contract(rows_landed[panel, block], spread[block])
        solved[panel] = total.astype(BF16)

    drain(diag_all.at[0, pl.ds(0, Z - 1)], near_recv.at[0])
    scatter(0, rhs_first)
    for block in range(Z):
        lane = lax.broadcasted_iota(jnp.int32, (width, nrhs), 0)
        target = lax.broadcasted_iota(jnp.int32, (width, nrhs), 1)
        spread[block] = (target == ((lane // share) * Z + block) * share + lane % share).astype(F32).astype(BF16)
    gather(0)
    ring_wait(1)
    ring_send(2)
    drain(cross_all.at[pl.ds(0, Z - 1)], near_recv.at[1])
    gathered(0)

    crossed = contract_rows(cross_all[...].reshape(Z * bc, br), panels[0])
    cross_sent[...] = crossed.astype(BF16)
    for d in range(1, X):
        send(cross_sent, cross_landed.at[d - 1], last_send.at[0], last_recv.at[0],
             (row, x_peer(d) * Z + z))
    spread_rows(0)
    drain(diag_all.at[1, pl.ds(0, Z - 1)], near_recv.at[2])
    drain(cross_landed, last_recv.at[0])
    for d in range(X - 1):
        crossed = crossed + cross_landed[d].astype(F32)
    reduced = (rhs_second - crossed).astype(BF16)

    scatter(1, reduced)
    ring_wait(2)
    ring_send(3)
    write_rows(0)
    gather(1)
    ring_wait(3)
    ring_send(4)
    ring_wait(4, (0,))
    update[...] = contract_rows(panels[0], trail_all[0].reshape(Z * bc, trail.shape[2]))
    gathered(1)
    spread_rows(1)

    ring_wait(4, (1,))
    total = update[...] + contract_rows(panels[1], trail_all[1].reshape(Z * bc, trail.shape[2]))
    update[...] = total
    update_sent[...] = total.astype(BF16).reshape(X, share, trail.shape[2])
    for d in range(1, X):
        send(update_sent.at[x_peer(d)], update_landed.at[d - 1], last_send.at[1], last_recv.at[1],
             (row, x_peer(d) * Z + z))
    write_rows(1)
    total = update[pl.ds(pl.multiple_of(x * share, share), share), :]
    drain(update_landed, last_recv.at[1])
    for d in range(X - 1):
        total = total + update_landed[d].astype(F32)
    new[...] = old[...] - total

    drain(diag_all.at[0, pl.ds(0, Z - 1)], near_send.at[0])
    drain(cross_all.at[pl.ds(0, Z - 1)], near_send.at[1])
    drain(diag_all.at[1, pl.ds(0, Z - 1)], near_send.at[2])
    ring_drain()
    for panel in range(2):
        drain(landed.at[panel], sum_send.at[panel, 0])
        drain(panels.at[panel, pl.ds(0, (R - 1) * piece), :], sum_send.at[panel, 1])
        drain(rows_landed.at[panel, pl.ds(0, Z - 1)], rows_send.at[panel])
    drain(cross_landed, last_send.at[0])
    drain(update_landed, last_send.at[1])


def build(mesh, X, Z):
    R = mesh.shape["row"]

    def per_device(panel_rhs, diag_inverse, cross_block, trail_factor, trail_rhs):
        _, br, nrhs = panel_rhs.shape
        bc = diag_inverse.shape[1]
        rows = trail_factor.shape[0]
        share = nrhs // (X * Z)
        width = share * X
        piece = Z * bc // R
        vmem = pl.BlockSpec(memory_space=pltpu.VMEM)
        solved, new = pl.pallas_call(
            functools.partial(kernel, R, X, Z),
            out_shape=(
                jax.ShapeDtypeStruct((2, bc, nrhs), BF16),
                jax.ShapeDtypeStruct((share, rows), F32),
            ),
            in_specs=[vmem, vmem, vmem, pl.BlockSpec(memory_space=pl.ANY), vmem],
            out_specs=(vmem, vmem),
            scratch_shapes=[
                pltpu.VMEM((2, Z, bc, rows), BF16),
                pltpu.VMEM((2, Z, bc, br), BF16),
                pltpu.VMEM((Z, bc, br), BF16),
                pltpu.VMEM((Z * bc, width), F32),
                pltpu.VMEM((2, R, piece, width), BF16),
                pltpu.VMEM((2, R - 1, piece, width), BF16),
                pltpu.VMEM((2, Z * bc, width), BF16),
                pltpu.VMEM((br, width), BF16),
                pltpu.VMEM((X - 1, br, width), BF16),
                pltpu.VMEM((width, rows), F32),
                pltpu.VMEM((X, share, rows), BF16),
                pltpu.VMEM((X - 1, share, rows), BF16),
                pltpu.VMEM((2, Z, bc, width), BF16),
                pltpu.VMEM((Z, width, nrhs), BF16),
                pltpu.SemaphoreType.DMA((1,)),
                pltpu.SemaphoreType.DMA((3,)),
                pltpu.SemaphoreType.DMA((3,)),
                pltpu.SemaphoreType.DMA((2, 2, Z // 2)),
                pltpu.SemaphoreType.DMA((2, 2, Z // 2)),
                pltpu.SemaphoreType.DMA((2, 2)),
                pltpu.SemaphoreType.DMA((2, 2)),
                pltpu.SemaphoreType.DMA((2,)),
                pltpu.SemaphoreType.DMA((2,)),
                pltpu.SemaphoreType.DMA((2,)),
                pltpu.SemaphoreType.DMA((2,)),
            ],
            compiler_params=pltpu.CompilerParams(
                collective_id=0, has_side_effects=True, vmem_limit_bytes=40 * 1024 * 1024
            ),
        )(
            panel_rhs,
            diag_inverse,
            cross_block.T,
            jnp.transpose(trail_factor, (1, 2, 0)),
            trail_rhs.T,
        )
        return solved, new.T

    in_specs = (
        P(None, "row", None),
        P(None, "col", "row"),
        P("row", "col"),
        P("row", None, "col"),
        P("row", "col"),
    )
    out_specs = (P(None, "col", None), P("row", "col"))
    return jax.shard_map(
        per_device, mesh=mesh, in_specs=in_specs, out_specs=out_specs, check_vma=False
    )


def solution(mesh):
    return build(mesh, 4, 8)
```

time: 501 us -> 67.1 us (0.13)
  the two profiles are of different devices: /device:TPU:1 before, /device:TPU:8 now
where the time goes in v1:
time: 67.1 us; the launch traced here: 66.7 us
  Pallas kernels  60.4 us (90%)
  local copies, waits for them, and re-layouts  5.72 us (9%)
    pallas_call x1, Pallas kernels, per_device(): pl.pallas_call(functools.partial(kernel, R, X, Z), out_shape=(jax.ShapeDt...  60.4 us
    unnamed x12, local copies, waits for them, and re-layouts  5.72 us

profile of v1, /device:TPU:8, one launch (start us, length us, event | category | flops | bytes accessed | tf_op | source)
XLA Modules:
  0.0 66.7 jit_solution(3431895329677791082)
XLA Ops:
  0.6 0.0 copy-start
  0.6 1.0 %copy-done = bf16[2,128,1024]{2,1,0:T(8,128)(2,1)S(1)} copy-done((bf16[2,128,1024]{2,1,0:T(8,128)(2,1)S(1)}, bf16[2,128,1024]{2,1,0:T(8,128)(2,1)}, u32[]{:S(2)}) %copy-start) | copy-done | bytes 524312
  1.7 0.0 copy-start.1
  1.7 0.9 %copy-done.1 = bf16[1024,2,64]{0,2,1:T(8,128)(2,1)S(1)} copy-done((bf16[1024,2,64]{0,2,1:T(8,128)(2,1)S(1)}, bf16[1024,2,64]{0,2,1:T(8,128)(2,1)}, u32[]{:S(2)}) %copy-start.1) | copy-done | bytes 262168
  2.6 0.0 copy-start.2
  2.6 0.9 %copy-done.2 = f32[1024,32]{0,1:T(8,128)S(1)} copy-done((f32[1024,32]{0,1:T(8,128)S(1)}, f32[1024,32]{0,1:T(8,128)}, u32[]{:S(2)}) %copy-start.2) | copy-done | bytes 131096
  3.5 0.0 copy-start.3
  3.5 0.8 %copy-done.3 = bf16[2,64,128]{2,1,0:T(8,128)(2,1)S(1)} copy-done((bf16[2,64,128]{2,1,0:T(8,128)(2,1)S(1)}, bf16[2,64,128]{2,1,0:T(8,128)(2,1)}, u32[]{:S(2)}) %copy-start.3) | copy-done | bytes 32792
  4.3 0.0 copy-start.4
  4.3 0.7 %copy-done.4 = bf16[128,64]{0,1:T(8,128)(2,1)S(1)} copy-done((bf16[128,64]{0,1:T(8,128)(2,1)S(1)}, bf16[128,64]{0,1:T(8,128)(2,1)}, u32[]{:S(2)}) %copy-start.4) | copy-done | bytes 16408
  5.0 60.4 %shard_map.68 = (bf16[2,64,1024]{2,1,0:T(8,128)(2,1)S(1)}, f32[32,1024]{1,0:T(8,128)S(1)}) custom-call(bf16[2,128,1024]{2,1,0:T(8,128)(2,1)S(1)} %copy-done, bf16[2,64,128]{2,1,0:T(8,128)(2,1)S(1)} %copy-done.3, bf16[64,128]{1,0:T(8,128)(2,1)S(1)} %bitcast.7, bf16[2,64,1024]{2,1,0:T(8,128)(2,1)S(1)} %bitcast.4, f32[32,1024]{1,0:T(8,128)S(1)} %bitcast.6), custom_call_target="tpu_custom_call" | custom-call | tf_op jit(solution)/shard_map/pallas_call | solution.py:232
  65.4 0.7 %copy.9 = bf16[2,64,1024]{2,1,0:T(8,128)(2,1)} copy(bf16[2,64,1024]{2,1,0:T(8,128)(2,1)S(1)} %get-tuple-element.8) | data formatting | bytes 524288
  66.1 0.7 copy.10
Async XLA Ops:
  0.6 1.0 %copy-start = (bf16[2,128,1024]{2,1,0:T(8,128)(2,1)S(1)}, bf16[2,128,1024]{2,1,0:T(8,128)(2,1)}, u32[]{:S(2)}) copy-start(bf16[2,128,1024]{2,1,0:T(8,128)(2,1)} %rhs.1) | copy-start | bytes 1572868
  1.7 0.9 %copy-start.1 = (bf16[1024,2,64]{0,2,1:T(8,128)(2,1)S(1)}, bf16[1024,2,64]{0,2,1:T(8,128)(2,1)}, u32[]{:S(2)}) copy-start(bf16[1024,2,64]{0,2,1:T(8,128)(2,1)} %param.8) | copy-start | bytes 786436
  2.6 0.9 %copy-start.2 = (f32[1024,32]{0,1:T(8,128)S(1)}, f32[1024,32]{0,1:T(8,128)}, u32[]{:S(2)}) copy-start(f32[1024,32]{0,1:T(8,128)} %param.9) | copy-start | bytes 393220
  3.5 0.8 %copy-start.3 = (bf16[2,64,128]{2,1,0:T(8,128)(2,1)S(1)}, bf16[2,64,128]{2,1,0:T(8,128)(2,1)}, u32[]{:S(2)}) copy-start(bf16[2,64,128]{2,1,0:T(8,128)(2,1)} %diag.1) | copy-start | bytes 98308
  4.3 0.7 %copy-start.4 = (bf16[128,64]{0,1:T(8,128)(2,1)S(1)}, bf16[128,64]{0,1:T(8,128)(2,1)}, u32[]{:S(2)}) copy-start(bf16[128,64]{0,1:T(8,128)(2,1)} %param.7) | copy-start | bytes 49156

commit v2 on v1

--- a/solution.py
+++ b/solution.py
@@ -22,29 +22,45 @@
 
 def kernel(
     R, X, Z,
-    rhs, diag, cross, trail, old,
+    rhs_hbm, diag_hbm, cross_hbm, trail_hbm, old_hbm,
     solved, new,
-    trail_all, diag_all, cross_all, partial, sent, landed, panels, cross_sent, cross_landed,
-    update, update_sent, update_landed, rows_landed, spread,
+    rhs, old, trail_all, diag_all, cross_all, partial, sent, landed, panels, cross_sent, cross_landed,
+    update, update_sent, update_landed, rows_landed, spread, cross_turned,
     local_sem, near_send, near_recv, trail_send, trail_recv, sum_send, sum_recv,
     rows_send, rows_recv, last_send, last_recv,
 ):
     row, col = lax.axis_index("row"), lax.axis_index("col")
     x, z = col // Z, lax.rem(col, Z)
-    bc, br = diag.shape[1:]
-    nrhs = rhs.shape[2]
+    bc, br = diag_hbm.shape[1:]
+    nrhs = rhs_hbm.shape[2]
+    rows = trail_hbm.shape[2]
     share = nrhs // (X * Z)
     width = share * X
     piece = Z * bc // R
 
-    def row_peer(d):
-        return lax.rem(row + d, R)
+    rings = R // 2
+    y, core = row // 2, lax.rem(row, 2)
+    row_steps = [
+        (dy, dc)
+        for dy in sorted(range(rings), key=lambda d: -min(d, rings - d))
+        for dc in range(2)
+        if dy or dc
+    ]
+    row_peers = [lax.rem(y + dy, rings) * 2 + lax.rem(core + dc, 2) for dy, dc in row_steps]
+    x_steps = sorted(range(1, X), key=lambda d: -min(d, X - d))
+    order = sorted(range(1, Z), key=lambda d: -min(d, Z - d))
 
     def x_peer(d):
         return lax.rem(x + d, X)
 
     def z_peer(d):
         return lax.rem(z + d + Z, Z)
+
+    bits = share.bit_length() - 1
+
+    def chosen(target, lane, block):
+        group = lax.shift_right_logical(lane, bits)
+        return (target == (group * Z + block) * share + (lane & (share - 1))).astype(F32).astype(BF16)
 
     def send(src, dst, send_sem, recv_sem, where):
         copy = pltpu.make_async_remote_copy(
@@ -56,30 +72,35 @@
     def drain(ref, sem):
         pltpu.make_async_copy(ref, ref, sem).wait()
 
-    trail_own = pltpu.make_async_copy(trail, trail_all.at[:, z], local_sem.at[0])
-    trail_own.start()
+    loads = [
+        pltpu.make_async_copy(src, dst, local_sem.at[i])
+        for i, (src, dst) in enumerate([
+            (rhs_hbm, rhs), (diag_hbm, diag_all.at[:, z]), (cross_hbm, cross_all.at[z]),
+            (trail_hbm, trail_all.at[:, z]), (old_hbm, old),
+        ])
+    ]
+    for load in loads:
+        load.start()
 
     barrier = pltpu.get_barrier_semaphore()
-    for d in range(1, R):
-        pl.semaphore_signal(barrier, inc=1, device_id=(row_peer(d), col), device_id_type=MESH)
-    for d in range(1, X):
+    for peer in row_peers:
+        pl.semaphore_signal(barrier, inc=1, device_id=(peer, col), device_id_type=MESH)
+    for d in x_steps:
         pl.semaphore_signal(barrier, inc=1, device_id=(row, x_peer(d) * Z + z), device_id_type=MESH)
-    for d in range(1, Z):
+    for d in order:
         pl.semaphore_signal(barrier, inc=1, device_id=(row, x * Z + z_peer(d)), device_id_type=MESH)
 
-    diag_all[0, z] = diag[0]
-    diag_all[1, z] = diag[1]
-    cross_all[z] = cross[...]
     source = lax.broadcasted_iota(jnp.int32, (nrhs, width), 0)
     lane = lax.broadcasted_iota(jnp.int32, (nrhs, width), 1)
-    pick = (source == ((lane // share) * Z + z) * share + lane % share).astype(F32).astype(BF16)
+    pick = chosen(source, lane, z)
+    loads[0].wait()
     rhs_first = contract(rhs[0], pick).astype(BF16)
     rhs_second = contract(rhs[1], pick)
-    trail_own.wait()
+    for load in loads[1:]:
+        load.wait()
 
     pl.semaphore_wait(barrier, (R - 1) + (X - 1) + (Z - 1))
 
-    order = sorted(range(1, Z), key=lambda d: -min(d, Z - d))
     for d in order:
         send(diag_all.at[0, z], diag_all.at[0, z], near_send.at[0], near_recv.at[0], (row, x * Z + z_peer(d)))
     for d in order:
@@ -123,9 +144,9 @@
         total = contract(diag_all[panel].reshape(Z * bc, br), right_side)
         partial[...] = total
         sent[panel] = total.astype(BF16).reshape(R, piece, width)
-        for d in range(1, R):
-            send(sent.at[panel, row_peer(d)], landed.at[panel, d - 1], sum_send.at[panel, 0],
-                 sum_recv.at[panel, 0], (row_peer(d), col))
+        for slot, peer in enumerate(row_peers):
+            send(sent.at[panel, peer], landed.at[panel, slot], sum_send.at[panel, 0],
+                 sum_recv.at[panel, 0], (peer, col))
 
     def gather(panel):
         drain(landed.at[panel], sum_recv.at[panel, 0])
@@ -134,9 +155,9 @@
         for d in range(R - 1):
             total = total + landed[panel, d].astype(F32)
         panels[panel, mine, :] = total.astype(BF16)
-        for d in range(1, R):
+        for peer in row_peers:
             send(panels.at[panel, mine, :], panels.at[panel, mine, :], sum_send.at[panel, 1],
-                 sum_recv.at[panel, 1], (row_peer(d), col))
+                 sum_recv.at[panel, 1], (peer, col))
 
     def gathered(panel):
         drain(panels.at[panel, pl.ds(0, (R - 1) * piece), :], sum_recv.at[panel, 1])
@@ -158,19 +179,24 @@
 
     drain(diag_all.at[0, pl.ds(0, Z - 1)], near_recv.at[0])
     scatter(0, rhs_first)
-    for block in range(Z):
-        lane = lax.broadcasted_iota(jnp.int32, (width, nrhs), 0)
-        target = lax.broadcasted_iota(jnp.int32, (width, nrhs), 1)
-        spread[block] = (target == ((lane // share) * Z + block) * share + lane % share).astype(F32).astype(BF16)
+    lane = lax.broadcasted_iota(jnp.int32, (width, nrhs), 0)
+    target = lax.broadcasted_iota(jnp.int32, (width, nrhs), 1)
+
+    def fill(block, _):
+        spread[block] = chosen(target, lane, block)
+        return 0
+
+    lax.fori_loop(0, Z, fill, 0)
     gather(0)
     ring_wait(1)
     ring_send(2)
     drain(cross_all.at[pl.ds(0, Z - 1)], near_recv.at[1])
+    cross_turned[...] = cross_all[...].reshape(Z * bc, br).T
     gathered(0)
 
-    crossed = contract_rows(cross_all[...].reshape(Z * bc, br), panels[0])
+    crossed = contract(cross_turned[...], panels[0])
     cross_sent[...] = crossed.astype(BF16)
-    for d in range(1, X):
+    for d in x_steps:
         send(cross_sent, cross_landed.at[d - 1], last_send.at[0], last_recv.at[0],
              (row, x_peer(d) * Z + z))
     spread_rows(0)
@@ -188,15 +214,15 @@
     ring_wait(3)
     ring_send(4)
     ring_wait(4, (0,))
-    update[...] = contract_rows(panels[0], trail_all[0].reshape(Z * bc, trail.shape[2]))
+    update[...] = contract_rows(panels[0], trail_all[0].reshape(Z * bc, rows))
     gathered(1)
     spread_rows(1)
 
     ring_wait(4, (1,))
-    total = update[...] + contract_rows(panels[1], trail_all[1].reshape(Z * bc, trail.shape[2]))
+    total = update[...] + contract_rows(panels[1], trail_all[1].reshape(Z * bc, rows))
     update[...] = total
-    update_sent[...] = total.astype(BF16).reshape(X, share, trail.shape[2])
-    for d in range(1, X):
+    update_sent[...] = total.astype(BF16).reshape(X, share, rows)
+    for d in x_steps:
         send(update_sent.at[x_peer(d)], update_landed.at[d - 1], last_send.at[1], last_recv.at[1],
              (row, x_peer(d) * Z + z))
     write_rows(1)
@@ -235,9 +261,11 @@
                 jax.ShapeDtypeStruct((2, bc, nrhs), BF16),
                 jax.ShapeDtypeStruct((share, rows), F32),
             ),
-            in_specs=[vmem, vmem, vmem, pl.BlockSpec(memory_space=pl.ANY), vmem],
+            in_specs=[pl.BlockSpec(memory_space=pltpu.HBM)] * 5,
             out_specs=(vmem, vmem),
             scratch_shapes=[
+                pltpu.VMEM((2, br, nrhs), BF16),
+                pltpu.VMEM((share, rows), F32),
                 pltpu.VMEM((2, Z, bc, rows), BF16),
                 pltpu.VMEM((2, Z, bc, br), BF16),
                 pltpu.VMEM((Z, bc, br), BF16),
@@ -252,7 +280,8 @@
                 pltpu.VMEM((X - 1, share, rows), BF16),
                 pltpu.VMEM((2, Z, bc, width), BF16),
                 pltpu.VMEM((Z, width, nrhs), BF16),
-                pltpu.SemaphoreType.DMA((1,)),
+                pltpu.VMEM((br, Z * bc), BF16),
+                pltpu.SemaphoreType.DMA((5,)),
                 pltpu.SemaphoreType.DMA((3,)),
                 pltpu.SemaphoreType.DMA((3,)),
                 pltpu.SemaphoreType.DMA((2, 2, Z // 2)),
@@ -265,7 +294,7 @@
                 pltpu.SemaphoreType.DMA((2,)),
             ],
             compiler_params=pltpu.CompilerParams(
-                collective_id=0, has_side_effects=True, vmem_limit_bytes=40 * 1024 * 1024
+                collective_id=0, has_side_effects=True, vmem_limit_bytes=63 * 1024 * 1024
             ),
         )(
             panel_rhs,

time: 67.1 us -> 63.4 us (0.945)
  local copies, waits for them, and re-layouts: 5.72 us -> 2.36 us
    unnamed x12 -> x4, local copies, waits for them, and re-layouts: 5.72 us -> 2.36 us
where the time goes in v2:
time: 63.4 us; the launch traced here: 63.2 us
  Pallas kernels  60.2 us (95%)
  local copies, waits for them, and re-layouts  2.36 us (4%)
  between operations  0.65 us (1%)
    pallas_call x1, Pallas kernels, per_device(): pl.pallas_call(functools.partial(kernel, R, X, Z), out_shape=(jax.ShapeDt...  60.2 us
    unnamed x4, local copies, waits for them, and re-layouts  2.36 us

profile of v2, /device:TPU:8, one launch (start us, length us, event | category | flops | bytes accessed | tf_op | source)
XLA Modules:
  0.0 63.2 jit_solution(4033302071053486399)
XLA Ops:
  0.6 60.2 %shard_map.68 = (bf16[2,64,1024]{2,1,0:T(8,128)(2,1)}, f32[32,1024]{1,0:T(8,128)}) custom-call(bf16[2,128,1024]{2,1,0:T(8,128)(2,1)} %rhs_hbm.1, bf16[2,64,128]{2,1,0:T(8,128)(2,1)} %diag_hbm.1, bf16[64,128]{1,0:T(8,128)(2,1)} %bitcast.7, bf16[2,64,1024]{2,1,0:T(8,128)(2,1)} %bitcast.4, f32[32,1024]{1,0:T(8,128)} %bitcast.6), custom_call_target="tpu_custom_call" | custom-call | tf_op jit(solution)/shard_map/pallas_call | solution.py:258
  60.9 0.0 copy-start
  60.9 1.7 %copy.9 = bf16[2,64,1024]{2,1,0:T(8,128)(2,1)} copy(bf16[2,64,1024]{2,1,0:T(8,128)(2,1)} %get-tuple-element.8) | data formatting | bytes 524288
  62.6 0.0 copy-done
  62.6 0.7 %copy.10 = f32[1024,32]{0,1:T(8,128)} copy(f32[1024,32]{0,1:T(8,128)S(1)} %bitcast.5) | data formatting | bytes 262144
Async XLA Ops:
  60.9 1.7 %copy-start = (f32[32,1024]{1,0:T(8,128)S(1)}, f32[32,1024]{1,0:T(8,128)}, u32[]{:S(2)}) copy-start(f32[32,1024]{1,0:T(8,128)} %get-tuple-element.5) | copy-start | bytes 393220

commit v3 on v2

v3 whole, which is shorter than its diff:
```python
import functools

import jax
import jax.numpy as jnp
from jax import lax
from jax.experimental import pallas as pl
from jax.experimental.pallas import tpu as pltpu
from jax.sharding import PartitionSpec as P

MESH = pl.DeviceIdType.MESH
BF16 = jnp.bfloat16
F32 = jnp.float32


def contract_rows(left, right):
    return lax.dot_general(left, right, (((0,), (0,)), ((), ())), preferred_element_type=F32)


def contract(left, right):
    return jnp.dot(left, right, preferred_element_type=F32)


def kernel(
    R, X, Z,
    rhs_hbm, diag_hbm, cross_hbm, trail_hbm, old_hbm,
    solved, new,
    rhs, old, trail_all, diag_first, diag_all, cross_all, partial, sent, landed, panels, cross_sent, cross_landed,
    update, update_sent, update_landed, rows_landed, cross_turned, first_sent, first_landed, first_own, first_piece, first_rows,
    local_sem, near_send, near_recv, trail_send, trail_recv, sum_send, sum_recv,
    rows_send, rows_recv, last_send, last_recv, first_send, first_recv,
):
    row, col = lax.axis_index("row"), lax.axis_index("col")
    x, z = col // Z, lax.rem(col, Z)
    bc, br = diag_hbm.shape[1:]
    nrhs = rhs_hbm.shape[2]
    rows = trail_hbm.shape[2]
    share = nrhs // (X * Z)
    width = share * X
    piece = Z * bc // R

    rings = R // 2
    y, core = row // 2, lax.rem(row, 2)
    row_steps = [
        (dy, dc)
        for dy in sorted(range(rings), key=lambda d: -min(d, rings - d))
        for dc in range(2)
        if dy or dc
    ]
    row_peers = [lax.rem(y + dy, rings) * 2 + lax.rem(core + dc, 2) for dy, dc in row_steps]
    x_steps = sorted(range(1, X), key=lambda d: -min(d, X - d))
    order = sorted(range(1, Z), key=lambda d: -min(d, Z - d))

    def x_peer(d):
        return lax.rem(x + d, X)

    def z_peer(d):
        return lax.rem(z + d + Z, Z)

    sets = Z // 2
    slabs = R // sets
    slab = bc // slabs
    my_set, my_slab = lax.rem(row, sets), row // sets
    first_peers = [row] + row_peers
    bits = share.bit_length() - 1

    def chosen(target, lane, block):
        group = lax.shift_right_logical(lane, bits)
        return (target == (group * Z + block) * share + (lane & (share - 1))).astype(F32).astype(BF16)

    def send(src, dst, send_sem, recv_sem, where):
        copy = pltpu.make_async_remote_copy(
            src_ref=src, dst_ref=dst, send_sem=send_sem, recv_sem=recv_sem,
            device_id=where, device_id_type=MESH,
        )
        copy.start()

    def drain(ref, sem):
        pltpu.make_async_copy(ref, ref, sem).wait()

    loads = [
        pltpu.make_async_copy(src, dst, local_sem.at[i])
        for i, (src, dst) in enumerate([
            (rhs_hbm, rhs), (diag_hbm.at[0], diag_first), (diag_hbm.at[1], diag_all.at[z]), (cross_hbm, cross_all.at[z]),
            (trail_hbm, trail_all.at[:, z]), (old_hbm, old),
        ])
    ]
    for load in loads:
        load.start()

    barrier = pltpu.get_barrier_semaphore()
    for peer in row_peers:
        pl.semaphore_signal(barrier, inc=1, device_id=(peer, col), device_id_type=MESH)
    for d in x_steps:
        pl.semaphore_signal(barrier, inc=1, device_id=(row, x_peer(d) * Z + z), device_id_type=MESH)
    for d in order:
        pl.semaphore_signal(barrier, inc=1, device_id=(row, x * Z + z_peer(d)), device_id_type=MESH)
    for block in range(Z):
        for index in range(slabs):
            giver = index * sets + lax.rem(z, sets)

            @pl.when(jnp.logical_or(giver != row, z != block))
            def _():
                pl.semaphore_signal(barrier, inc=1, device_id=(giver, x * Z + block), device_id_type=MESH)

    at_home = (my_set == lax.rem(z, sets)).astype(jnp.int32)

    loads[0].wait()
    place = lax.shift_right_logical(lax.broadcasted_iota(jnp.int32, (br, width), 1), bits)
    tiles = [rhs[0, :, tile * width:(tile + 1) * width].astype(F32) for tile in range(Z)]
    loads[1].wait()
    for block in range(Z):
        mixed = None
        for group in range(X):
            tile, q = divmod(group * Z + block, X)
            shift = (group - q) % X * share
            moved = pltpu.roll(tiles[tile], shift, 1) if shift else tiles[tile]
            mixed = moved if mixed is None else jnp.where(place == group, moved, mixed)
        product = contract(diag_first[...], mixed.astype(BF16))
        rounded = product.astype(BF16)
        for index in range(slabs):
            first_own[index * sets + block % sets, block // sets] = product[index * slab:(index + 1) * slab]
            first_sent[index * sets + block % sets, block // sets] = rounded[index * slab:(index + 1) * slab]

    pl.semaphore_wait(barrier, (R - 1) + (X - 1) + (Z - 1) + 2 * R - at_home)

    for slot, peer in enumerate(row_peers):
        send(first_sent.at[peer], first_landed.at[slot], first_send.at[0], first_recv.at[0], (peer, col))
    for load in loads[2:]:
        load.wait()
    for d in (2, -2, 1, -1):
        for which, buffer in enumerate((cross_all, diag_all)):
            send(buffer.at[z], buffer.at[z], near_send.at[0], near_recv.at[0 if abs(d) == 2 else 1 + which],
                 (row, x * Z + z_peer(d)))

    def pass_on():
        drain(cross_all.at[pl.ds(0, 4)], near_recv.at[0])
        for which, buffer in enumerate((cross_all, diag_all)):
            for sign in (1, -1):
                block = z_peer(-2 * sign)
                part = pl.ds(0 if sign == 1 else bc // 2, bc // 2)
                send(buffer.at[block], buffer.at[block], near_send.at[0], near_recv.at[1 + which],
                     (row, x * Z + z_peer(sign)))
                send(buffer.at[block, part, :], buffer.at[block, part, :], near_send.at[0], near_recv.at[1 + which],
                     (row, x * Z + z_peer(2 * sign)))

    half = Z // 2

    def ring_has(way, panel, step):
        return step < half or (step == half and way == panel)

    def ring_send(step, panel, way):
        if ring_has(way, panel, step):
            sign = 1 - 2 * way
            block = z_peer(-sign * (step - 1))
            send(
                trail_all.at[panel, block], trail_all.at[panel, block],
                trail_send.at[way, panel, step - 1], trail_recv.at[way, panel, step - 1],
                (row, x * Z + z_peer(sign)),
            )

    def ring_wait(step, panel, way):
        if ring_has(way, panel, step):
            drain(trail_all.at[panel, 0], trail_recv.at[way, panel, step - 1])

    def ring_pass(step):
        for panel in range(2):
            for way in range(2):
                ring_wait(step, panel, way)
                ring_send(step + 1, panel, way)

    def ring_drain():
        for step in range(1, half + 1):
            for panel in range(2):
                for way in range(2):
                    if ring_has(way, panel, step):
                        drain(trail_all.at[panel, 0], trail_send.at[way, panel, step - 1])

    for panel in range(2):
        for way in range(2):
            ring_send(1, panel, way)

    def scatter(panel, right_side):
        total = contract(diag_all[...].reshape(Z * bc, br), right_side)
        partial[...] = total
        sent[...] = total.astype(BF16).reshape(R, piece, width)
        for slot, peer in enumerate(row_peers):
            send(sent.at[peer], landed.at[slot], sum_send.at[0],
                 sum_recv.at[0], (peer, col))

    def gather(panel):
        drain(landed, sum_recv.at[0])
        mine = pl.ds(pl.multiple_of(row * piece, piece), piece)
        total = partial[mine, :]
        for d in range(R - 1):
            total = total + landed[d].astype(F32)
        panels[panel, mine, :] = total.astype(BF16)
        for peer in row_peers:
            send(panels.at[panel, mine, :], panels.at[panel, mine, :], sum_send.at[1],
                 sum_recv.at[1], (peer, col))

    def gathered(panel):
        drain(panels.at[panel, pl.ds(0, (R - 1) * piece), :], sum_recv.at[1])

    def spread_rows(panel):
        own = panels[panel, pl.ds(pl.multiple_of(z * bc, bc), bc), :]
        rows_landed[z] = own
        for d in order:
            theirs = pl.ds(pl.multiple_of(z_peer(d) * bc, bc), bc)
            send(panels.at[panel, theirs, :], rows_landed.at[z], rows_send.at[0],
                 rows_recv.at[0], (row, x * Z + z_peer(d)))

    def write_rows(panel, blocks):
        place = lax.shift_right_logical(lax.broadcasted_iota(jnp.int32, (bc, width), 1), bits)
        for tile in range(Z):
            group, first = divmod(tile * X, Z)
            out = None
            for q in range(X):
                shift = (q - group) % X * share
                moved = pltpu.roll(blocks[first + q], shift, 1) if shift else blocks[first + q]
                out = moved if out is None else jnp.where(place == q, moved, out)
            solved[panel, :, tile * width:(tile + 1) * width] = out.astype(BF16)

    source = lax.broadcasted_iota(jnp.int32, (nrhs, width), 0)
    lane = lax.broadcasted_iota(jnp.int32, (nrhs, width), 1)
    rhs_second = contract(rhs[1], chosen(source, lane, z))
    drain(first_landed, first_recv.at[0])
    total = first_own[row]
    for slot in range(R - 1):
        total = total + first_landed[slot].astype(F32)
    first_piece[...] = total.astype(BF16)
    first_place = pl.ds(pl.multiple_of(z * bc + my_slab * slab, slab), slab)
    for which, peer in enumerate([*row_peers, row]):
        for side in range(2):
            block = my_set + side * sets
            target = panels.at[0, first_place, :]
            if which < R - 1:
                send(first_piece.at[side], target, first_send.at[1], first_recv.at[1], (peer, x * Z + block))
            else:
                @pl.when(block != z)
                def _():
                    send(first_piece.at[side], target, first_send.at[1], first_recv.at[1], (row, x * Z + block))

                @pl.when(block == z)
                def _():
                    pltpu.make_async_copy(first_piece.at[side], target, first_recv.at[1]).start()
    first_rows[row] = first_piece[...]
    pass_on()
    for peer in row_peers:
        send(first_piece, first_rows.at[row], first_send.at[2], first_recv.at[2], (peer, col))
    ring_pass(1)
    drain(cross_all.at[pl.ds(0, Z - 3)], near_recv.at[1])
    cross_turned[...] = cross_all[...].reshape(Z * bc, br).T
    drain(panels.at[0], first_recv.at[1])

    crossed = contract(cross_turned[...], panels[0])
    cross_sent[...] = crossed.astype(BF16)
    for d in x_steps:
        send(cross_sent, cross_landed.at[d - 1], last_send.at[0], last_recv.at[0],
             (row, x_peer(d) * Z + z))
    if half > 2:
        ring_pass(2)
    drain(diag_all.at[pl.ds(0, Z - 3)], near_recv.at[2])
    drain(cross_landed, last_recv.at[0])
    for d in range(X - 1):
        crossed = crossed + cross_landed[d].astype(F32)
    reduced = (rhs_second - crossed).astype(BF16)

    scatter(1, reduced)
    for step in range(3, half):
        ring_pass(step)
    gather(1)
    ring_wait(half, 0, 0)
    update[...] = contract_rows(panels[0], trail_all[0].reshape(Z * bc, rows))
    gathered(1)
    spread_rows(1)

    ring_wait(half, 1, 1)
    total = update[...] + contract_rows(panels[1], trail_all[1].reshape(Z * bc, rows))
    update[...] = total
    update_sent[...] = total.astype(BF16).reshape(X, share, rows)
    for d in x_steps:
        send(update_sent.at[x_peer(d)], update_landed.at[d - 1], last_send.at[1], last_recv.at[1],
             (row, x_peer(d) * Z + z))
    drain(first_rows.at[pl.ds(0, R - 1)], first_recv.at[2])
    write_rows(0, [
        jnp.concatenate([first_rows[index * sets + block % sets, block // sets].astype(F32) for index in range(slabs)], axis=0)
        for block in range(Z)
    ])
    total = update[pl.ds(pl.multiple_of(x * share, share), share), :]
    drain(update_landed, last_recv.at[1])
    for d in range(X - 1):
        total = total + update_landed[d].astype(F32)
    new[...] = old[...] - total
    drain(rows_landed.at[pl.ds(0, Z - 1)], rows_recv.at[0])
    write_rows(1, [rows_landed[block].astype(F32) for block in range(Z)])

    drain(first_landed, first_send.at[0])
    drain(panels.at[0, pl.ds(0, (R - 1) * 2 * slab), :], first_send.at[1])
    for side in range(2):
        @pl.when(my_set + side * sets != z)
        def _():
            drain(first_piece.at[side], first_send.at[1])
    drain(first_rows.at[pl.ds(0, R - 1)], first_send.at[2])
    for buffer in (cross_all, diag_all):
        drain(buffer.at[pl.ds(0, Z - 1)], near_send.at[0])
    ring_drain()
    drain(landed, sum_send.at[0])
    drain(panels.at[1, pl.ds(0, (R - 1) * piece), :], sum_send.at[1])
    drain(rows_landed.at[pl.ds(0, Z - 1)], rows_send.at[0])
    drain(cross_landed, last_send.at[0])
    drain(update_landed, last_send.at[1])


def build(mesh, X, Z):
    R = mesh.shape["row"]

    def per_device(panel_rhs, diag_inverse, cross_block, trail_factor, trail_rhs):
        _, br, nrhs = panel_rhs.shape
        bc = diag_inverse.shape[1]
        rows = trail_factor.shape[0]
        share = nrhs // (X * Z)
        width = share * X
        piece = Z * bc // R
        slab = bc // (R // (Z // 2))
        vmem = pl.BlockSpec(memory_space=pltpu.VMEM)
        solved, new = pl.pallas_call(
            functools.partial(kernel, R, X, Z),
            out_shape=(
                jax.ShapeDtypeStruct((2, bc, nrhs), BF16),
                jax.ShapeDtypeStruct((share, rows), F32),
            ),
            in_specs=[pl.BlockSpec(memory_space=pltpu.HBM)] * 5,
            out_specs=(vmem, vmem),
            scratch_shapes=[
                pltpu.VMEM((2, br, nrhs), BF16),
                pltpu.VMEM((share, rows), F32),
                pltpu.VMEM((2, Z, bc, rows), BF16),
                pltpu.VMEM((bc, br), BF16),
                pltpu.VMEM((Z, bc, br), BF16),
                pltpu.VMEM((Z, bc, br), BF16),
                pltpu.VMEM((Z * bc, width), F32),
                pltpu.VMEM((R, piece, width), BF16),
                pltpu.VMEM((R - 1, piece, width), BF16),
                pltpu.VMEM((2, Z * bc, width), BF16),
                pltpu.VMEM((br, width), BF16),
                pltpu.VMEM((X - 1, br, width), BF16),
                pltpu.VMEM((width, rows), F32),
                pltpu.VMEM((X, share, rows), BF16),
                pltpu.VMEM((X - 1, share, rows), BF16),
                pltpu.VMEM((Z, bc, width), BF16),
                pltpu.VMEM((br, Z * bc), BF16),
                pltpu.VMEM((R, 2, slab, width), BF16),
                pltpu.VMEM((R - 1, 2, slab, width), BF16),
                pltpu.VMEM((R, 2, slab, width), F32),
                pltpu.VMEM((2, slab, width), BF16),
                pltpu.VMEM((R, 2, slab, width), BF16),
                pltpu.SemaphoreType.DMA((6,)),
                pltpu.SemaphoreType.DMA((1,)),
                pltpu.SemaphoreType.DMA((3,)),
                pltpu.SemaphoreType.DMA((2, 2, Z // 2)),
                pltpu.SemaphoreType.DMA((2, 2, Z // 2)),
                pltpu.SemaphoreType.DMA((2,)),
                pltpu.SemaphoreType.DMA((2,)),
                pltpu.SemaphoreType.DMA((1,)),
                pltpu.SemaphoreType.DMA((1,)),
                pltpu.SemaphoreType.DMA((2,)),
                pltpu.SemaphoreType.DMA((2,)),
                pltpu.SemaphoreType.DMA((3,)),
                pltpu.SemaphoreType.DMA((3,)),
            ],
            compiler_params=pltpu.CompilerParams(
                collective_id=0, has_side_effects=True, vmem_limit_bytes=63 * 1024 * 1024
            ),
        )(
            panel_rhs,
            diag_inverse,
            cross_block.T,
            jnp.transpose(trail_factor, (1, 2, 0)),
            trail_rhs.T,
        )
        return solved, new.T

    in_specs = (
        P(None, "row", None),
        P(None, "col", "row"),
        P("row", "col"),
        P("row", None, "col"),
        P("row", "col"),
    )
    out_specs = (P(None, "col", None), P("row", "col"))
    return jax.shard_map(
        per_device, mesh=mesh, in_specs=in_specs, out_specs=out_specs, check_vma=False
    )


def solution(mesh):
    return build(mesh, 4, 8)
```

time: 63.4 us -> 58.3 us (0.920)
  the two profiles are of different devices: /device:TPU:8 before, /device:TPU:1 now
where the time goes in v3:
time: 58.3 us; the launch traced here: 58.1 us
  Pallas kernels  55.1 us (95%)
  local copies, waits for them, and re-layouts  2.36 us (4%)
  between operations  0.65 us (1%)
    pallas_call x1, Pallas kernels, per_device(): pl.pallas_call(functools.partial(kernel, R, X, Z), out_shape=(jax.ShapeDt...  55.1 us
    unnamed x4, local copies, waits for them, and re-layouts  2.36 us

profile of v3, /device:TPU:1, one launch (start us, length us, event | category | flops | bytes accessed | tf_op | source)
XLA Modules:
  0.0 58.1 jit_solution(5971161480587142072)
XLA Ops:
  0.6 55.1 %shard_map.68 = (bf16[2,64,1024]{2,1,0:T(8,128)(2,1)}, f32[32,1024]{1,0:T(8,128)}) custom-call(bf16[2,128,1024]{2,1,0:T(8,128)(2,1)} %rhs_hbm.1, bf16[2,64,128]{2,1,0:T(8,128)(2,1)} %diag_hbm.1, bf16[64,128]{1,0:T(8,128)(2,1)} %bitcast.7, bf16[2,64,1024]{2,1,0:T(8,128)(2,1)} %bitcast.4, f32[32,1024]{1,0:T(8,128)} %bitcast.6), custom_call_target="tpu_custom_call" | custom-call | tf_op jit(solution)/shard_map/pallas_call | solution.py:326
  55.7 0.0 copy-start
  55.8 1.7 %copy.9 = bf16[2,64,1024]{2,1,0:T(8,128)(2,1)} copy(bf16[2,64,1024]{2,1,0:T(8,128)(2,1)} %get-tuple-element.8) | data formatting | bytes 524288
  57.5 0.0 copy-done
  57.5 0.7 %copy.10 = f32[1024,32]{0,1:T(8,128)} copy(f32[1024,32]{0,1:T(8,128)S(1)} %bitcast.5) | data formatting | bytes 262144
Async XLA Ops:
  55.7 1.7 %copy-start = (f32[32,1024]{1,0:T(8,128)S(1)}, f32[32,1024]{1,0:T(8,128)}, u32[]{:S(2)}) copy-start(f32[32,1024]{1,0:T(8,128)} %get-tuple-element.5) | copy-start | bytes 393220

commit v4 on v3

--- a/solution.py
+++ b/solution.py
@@ -77,6 +77,17 @@
     def drain(ref, sem):
         pltpu.make_async_copy(ref, ref, sem).wait()
 
+    barrier = pltpu.get_barrier_semaphore()
+    for d in order:
+        for index in range(slabs):
+            giver = index * sets + lax.rem(z, sets)
+            pl.semaphore_signal(barrier, inc=1, device_id=(giver, x * Z + z_peer(d)), device_id_type=MESH)
+    for d in order:
+        pl.semaphore_signal(barrier, inc=1, device_id=(row, x * Z + z_peer(d)), device_id_type=MESH)
+    for peer in row_peers:
+        pl.semaphore_signal(barrier, inc=1, device_id=(peer, col), device_id_type=MESH)
+    for d in x_steps:
+        pl.semaphore_signal(barrier, inc=1, device_id=(row, x_peer(d) * Z + z), device_id_type=MESH)
     loads = [
         pltpu.make_async_copy(src, dst, local_sem.at[i])
         for i, (src, dst) in enumerate([
@@ -86,22 +97,6 @@
     ]
     for load in loads:
         load.start()
-
-    barrier = pltpu.get_barrier_semaphore()
-    for peer in row_peers:
-        pl.semaphore_signal(barrier, inc=1, device_id=(peer, col), device_id_type=MESH)
-    for d in x_steps:
-        pl.semaphore_signal(barrier, inc=1, device_id=(row, x_peer(d) * Z + z), device_id_type=MESH)
-    for d in order:
-        pl.semaphore_signal(barrier, inc=1, device_id=(row, x * Z + z_peer(d)), device_id_type=MESH)
-    for block in range(Z):
-        for index in range(slabs):
-            giver = index * sets + lax.rem(z, sets)
-
-            @pl.when(jnp.logical_or(giver != row, z != block))
-            def _():
-                pl.semaphore_signal(barrier, inc=1, device_id=(giver, x * Z + block), device_id_type=MESH)
-
     at_home = (my_set == lax.rem(z, sets)).astype(jnp.int32)
 
     loads[0].wait()
@@ -121,7 +116,7 @@
             first_own[index * sets + block % sets, block // sets] = product[index * slab:(index + 1) * slab]
             first_sent[index * sets + block % sets, block // sets] = rounded[index * slab:(index + 1) * slab]
 
-    pl.semaphore_wait(barrier, (R - 1) + (X - 1) + (Z - 1) + 2 * R - at_home)
+    pl.semaphore_wait(barrier, (R - 1) + (X - 1) + (Z - 1) + (2 - at_home) * R)
 
     for slot, peer in enumerate(row_peers):
         send(first_sent.at[peer], first_landed.at[slot], first_send.at[0], first_recv.at[0], (peer, col))
@@ -162,8 +157,8 @@
         if ring_has(way, panel, step):
             drain(trail_all.at[panel, 0], trail_recv.at[way, panel, step - 1])
 
-    def ring_pass(step):
-        for panel in range(2):
+    def ring_pass(step, which=(0, 1)):
+        for panel in which:
             for way in range(2):
                 ring_wait(step, panel, way)
                 ring_send(step + 1, panel, way)
@@ -243,10 +238,7 @@
                 @pl.when(block == z)
                 def _():
                     pltpu.make_async_copy(first_piece.at[side], target, first_recv.at[1]).start()
-    first_rows[row] = first_piece[...]
     pass_on()
-    for peer in row_peers:
-        send(first_piece, first_rows.at[row], first_send.at[2], first_recv.at[2], (peer, col))
     ring_pass(1)
     drain(cross_all.at[pl.ds(0, Z - 3)], near_recv.at[1])
     cross_turned[...] = cross_all[...].reshape(Z * bc, br).T
@@ -257,8 +249,10 @@
     for d in x_steps:
         send(cross_sent, cross_landed.at[d - 1], last_send.at[0], last_recv.at[0],
              (row, x_peer(d) * Z + z))
-    if half > 2:
-        ring_pass(2)
+    first_rows[row] = first_piece[...]
+    for peer in row_peers:
+        send(first_piece, first_rows.at[row], first_send.at[2], first_recv.at[2], (peer, col))
+    ring_pass(2, (0,))
     drain(diag_all.at[pl.ds(0, Z - 3)], near_recv.at[2])
     drain(cross_landed, last_recv.at[0])
     for d in range(X - 1):
@@ -266,6 +260,7 @@
     reduced = (rhs_second - crossed).astype(BF16)
 
     scatter(1, reduced)
+    ring_pass(2, (1,))
     for step in range(3, half):
         ring_pass(step)
     gather(1)
@@ -275,22 +270,28 @@
     spread_rows(1)
 
     ring_wait(half, 1, 1)
-    total = update[...] + contract_rows(panels[1], trail_all[1].reshape(Z * bc, rows))
-    update[...] = total
-    update_sent[...] = total.astype(BF16).reshape(X, share, rows)
-    for d in x_steps:
-        send(update_sent.at[x_peer(d)], update_landed.at[d - 1], last_send.at[1], last_recv.at[1],
-             (row, x_peer(d) * Z + z))
+    parts = 2
+    part = rows // parts
+    for index in range(parts):
+        lanes = pl.ds(index * part, part)
+        total = update[:, lanes] + contract_rows(panels[1], trail_all[1, :, :, lanes].reshape(Z * bc, part))
+        update[:, lanes] = total
+        update_sent[index] = total.astype(BF16).reshape(X, share, part)
+        for slot, d in enumerate(x_steps):
+            send(update_sent.at[index, x_peer(d)], update_landed.at[index, slot], last_send.at[1 + index],
+                 last_recv.at[1 + index], (row, x_peer(d) * Z + z))
     drain(first_rows.at[pl.ds(0, R - 1)], first_recv.at[2])
     write_rows(0, [
         jnp.concatenate([first_rows[index * sets + block % sets, block // sets].astype(F32) for index in range(slabs)], axis=0)
         for block in range(Z)
     ])
-    total = update[pl.ds(pl.multiple_of(x * share, share), share), :]
-    drain(update_landed, last_recv.at[1])
-    for d in range(X - 1):
-        total = total + update_landed[d].astype(F32)
-    new[...] = old[...] - total
+    for index in range(parts):
+        lanes = pl.ds(index * part, part)
+        total = update[pl.ds(pl.multiple_of(x * share, share), share), lanes]
+        drain(update_landed.at[index], last_recv.at[1 + index])
+        for slot in range(X - 1):
+            total = total + update_landed[index, slot].astype(F32)
+        new[:, lanes] = old[:, lanes] - total
     drain(rows_landed.at[pl.ds(0, Z - 1)], rows_recv.at[0])
     write_rows(1, [rows_landed[block].astype(F32) for block in range(Z)])
 
@@ -308,7 +309,8 @@
     drain(panels.at[1, pl.ds(0, (R - 1) * piece), :], sum_send.at[1])
     drain(rows_landed.at[pl.ds(0, Z - 1)], rows_send.at[0])
     drain(cross_landed, last_send.at[0])
-    drain(update_landed, last_send.at[1])
+    for index in range(parts):
+        drain(update_landed.at[index], last_send.at[1 + index])
 
 
 def build(mesh, X, Z):
@@ -326,8 +328,8 @@
         solved, new = pl.pallas_call(
             functools.partial(kernel, R, X, Z),
             out_shape=(
-                jax.ShapeDtypeStruct((2, bc, nrhs), BF16),
-                jax.ShapeDtypeStruct((share, rows), F32),
+                pltpu.VMEM((2, bc, nrhs), BF16),
+                pltpu.VMEM((share, rows), F32),
             ),
             in_specs=[pl.BlockSpec(memory_space=pltpu.HBM)] * 5,
             out_specs=(vmem, vmem),
@@ -345,8 +347,8 @@
                 pltpu.VMEM((br, width), BF16),
                 pltpu.VMEM((X - 1, br, width), BF16),
                 pltpu.VMEM((width, rows), F32),
-                pltpu.VMEM((X, share, rows), BF16),
-                pltpu.VMEM((X - 1, share, rows), BF16),
+                pltpu.VMEM((2, X, share, rows // 2), BF16),
+                pltpu.VMEM((2, X - 1, share, rows // 2), BF16),
                 pltpu.VMEM((Z, bc, width), BF16),
                 pltpu.VMEM((br, Z * bc), BF16),
                 pltpu.VMEM((R, 2, slab, width), BF16),
@@ -363,8 +365,8 @@
                 pltpu.SemaphoreType.DMA((2,)),
                 pltpu.SemaphoreType.DMA((1,)),
                 pltpu.SemaphoreType.DMA((1,)),
-                pltpu.SemaphoreType.DMA((2,)),
-                pltpu.SemaphoreType.DMA((2,)),
+                pltpu.SemaphoreType.DMA((3,)),
+                pltpu.SemaphoreType.DMA((3,)),
                 pltpu.SemaphoreType.DMA((3,)),
                 pltpu.SemaphoreType.DMA((3,)),
             ],

time: 58.3 us -> 54.8 us (0.940)
  Pallas kernels: 55.1 us -> 52.7 us
  local copies, waits for them, and re-layouts: 2.36 us -> 1.36 us
    pallas_call x1, Pallas kernels: 55.1 us -> 52.7 us  [per_device(): pl.pallas_call(functools.partial(kernel, R, X, Z), out_shape=(pltpu.VMEM(...]
    unnamed x4 -> x2, local copies, waits for them, and re-layouts: 2.36 us -> 1.36 us
where the time goes in v4:
time: 54.8 us; the launch traced here: 54.7 us
  Pallas kernels  52.7 us (96%)
  local copies, waits for them, and re-layouts  1.36 us (2%)
  between operations  0.64 us (1%)
    pallas_call x1, Pallas kernels, per_device(): pl.pallas_call(functools.partial(kernel, R, X, Z), out_shape=(pltpu.VMEM(...  52.7 us
    unnamed x2, local copies, waits for them, and re-layouts  1.36 us

profile of v4, /device:TPU:1, one launch (start us, length us, event | category | flops | bytes accessed | tf_op | source)
XLA Modules:
  0.0 54.7 jit_solution(9024071176237904175)
XLA Ops:
  0.6 52.7 %shard_map.68 = (bf16[2,64,1024]{2,1,0:T(8,128)(2,1)S(1)}, f32[32,1024]{1,0:T(8,128)S(1)}) custom-call(bf16[2,128,1024]{2,1,0:T(8,128)(2,1)} %rhs_hbm.1, bf16[2,64,128]{2,1,0:T(8,128)(2,1)} %diag_hbm.1, bf16[64,128]{1,0:T(8,128)(2,1)} %bitcast.7, bf16[2,64,1024]{2,1,0:T(8,128)(2,1)} %bitcast.5, f32[32,1024]{1,0:T(8,128)} %bitcast.6), custom_call_target="tpu_custom_call" | custom-call | tf_op jit(solution)/shard_map/pallas_call | solution.py:328
  53.3 0.7 %copy.9 = bf16[2,64,1024]{2,1,0:T(8,128)(2,1)} copy(bf16[2,64,1024]{2,1,0:T(8,128)(2,1)S(1)} %get-tuple-element.6) | data formatting | bytes 524288
  54.0 0.7 %copy.10 = f32[1024,32]{0,1:T(8,128)} copy(f32[1024,32]{0,1:T(8,128)S(1)} %bitcast.4) | data formatting | bytes 262144

commit v5 on v4

--- a/solution.py
+++ b/solution.py
@@ -77,6 +77,15 @@
     def drain(ref, sem):
         pltpu.make_async_copy(ref, ref, sem).wait()
 
+    loads = [
+        pltpu.make_async_copy(src, dst, local_sem.at[i])
+        for i, (src, dst) in enumerate([
+            (rhs_hbm, rhs), (diag_hbm.at[0], diag_first), (diag_hbm.at[1], diag_all.at[z]), (cross_hbm, cross_all.at[z]),
+            (trail_hbm, trail_all.at[:, z]), (old_hbm, old),
+        ])
+    ]
+    for load in loads:
+        load.start()
     barrier = pltpu.get_barrier_semaphore()
     for d in order:
         for index in range(slabs):
@@ -88,15 +97,6 @@
         pl.semaphore_signal(barrier, inc=1, device_id=(peer, col), device_id_type=MESH)
     for d in x_steps:
         pl.semaphore_signal(barrier, inc=1, device_id=(row, x_peer(d) * Z + z), device_id_type=MESH)
-    loads = [
-        pltpu.make_async_copy(src, dst, local_sem.at[i])
-        for i, (src, dst) in enumerate([
-            (rhs_hbm, rhs), (diag_hbm.at[0], diag_first), (diag_hbm.at[1], diag_all.at[z]), (cross_hbm, cross_all.at[z]),
-            (trail_hbm, trail_all.at[:, z]), (old_hbm, old),
-        ])
-    ]
-    for load in loads:
-        load.start()
     at_home = (my_set == lax.rem(z, sets)).astype(jnp.int32)
 
     loads[0].wait()
@@ -270,11 +270,12 @@
     spread_rows(1)
 
     ring_wait(half, 1, 1)
+    second_turned = panels[1].T
     parts = 2
     part = rows // parts
     for index in range(parts):
         lanes = pl.ds(index * part, part)
-        total = update[:, lanes] + contract_rows(panels[1], trail_all[1, :, :, lanes].reshape(Z * bc, part))
+        total = update[:, lanes] + contract(second_turned, trail_all[1, :, :, lanes].reshape(Z * bc, part))
         update[:, lanes] = total
         update_sent[index] = total.astype(BF16).reshape(X, share, part)
         for slot, d in enumerate(x_steps):

time: 54.8 us -> 54.8 us (level)
  no operation moved by 1% of the time
where the time goes in v5:
time: 54.8 us; the launch traced here: 54.7 us
  Pallas kernels  52.7 us (96%)
  local copies, waits for them, and re-layouts  1.36 us (2%)
  between operations  0.64 us (1%)
    pallas_call x1, Pallas kernels, per_device(): pl.pallas_call(functools.partial(kernel, R, X, Z), out_shape=(pltpu.VMEM(...  52.7 us
    unnamed x2, local copies, waits for them, and re-layouts  1.36 us

profile of v5, /device:TPU:1, one launch (start us, length us, event | category | flops | bytes accessed | tf_op | source)
XLA Modules:
  0.0 54.7 jit_solution(9267362818639954508)
XLA Ops:
  0.6 52.7 %shard_map.68 = (bf16[2,64,1024]{2,1,0:T(8,128)(2,1)S(1)}, f32[32,1024]{1,0:T(8,128)S(1)}) custom-call(bf16[2,128,1024]{2,1,0:T(8,128)(2,1)} %rhs_hbm.1, bf16[2,64,128]{2,1,0:T(8,128)(2,1)} %diag_hbm.1, bf16[64,128]{1,0:T(8,128)(2,1)} %bitcast.7, bf16[2,64,1024]{2,1,0:T(8,128)(2,1)} %bitcast.5, f32[32,1024]{1,0:T(8,128)} %bitcast.6), custom_call_target="tpu_custom_call" | custom-call | tf_op jit(solution)/shard_map/pallas_call | solution.py:329
  53.3 0.7 %copy.9 = bf16[2,64,1024]{2,1,0:T(8,128)(2,1)} copy(bf16[2,64,1024]{2,1,0:T(8,128)(2,1)S(1)} %get-tuple-element.6) | data formatting | bytes 524288
  54.0 0.7 %copy.10 = f32[1024,32]{0,1:T(8,128)} copy(f32[1024,32]{0,1:T(8,128)S(1)} %bitcast.4) | data formatting | bytes 262144

commit v6 on v5

--- a/solution.py
+++ b/solution.py
@@ -122,21 +122,20 @@
         send(first_sent.at[peer], first_landed.at[slot], first_send.at[0], first_recv.at[0], (peer, col))
     for load in loads[2:]:
         load.wait()
-    for d in (2, -2, 1, -1):
-        for which, buffer in enumerate((cross_all, diag_all)):
-            send(buffer.at[z], buffer.at[z], near_send.at[0], near_recv.at[0 if abs(d) == 2 else 1 + which],
+    for which, buffer in enumerate((cross_all, diag_all)):
+        for d in (2, -2, 1, -1):
+            send(buffer.at[z], buffer.at[z], near_send.at[0], near_recv.at[which + (2 if abs(d) == 2 else 0)],
                  (row, x * Z + z_peer(d)))
 
-    def pass_on():
-        drain(cross_all.at[pl.ds(0, 4)], near_recv.at[0])
-        for which, buffer in enumerate((cross_all, diag_all)):
-            for sign in (1, -1):
-                block = z_peer(-2 * sign)
-                part = pl.ds(0 if sign == 1 else bc // 2, bc // 2)
-                send(buffer.at[block], buffer.at[block], near_send.at[0], near_recv.at[1 + which],
-                     (row, x * Z + z_peer(sign)))
-                send(buffer.at[block, part, :], buffer.at[block, part, :], near_send.at[0], near_recv.at[1 + which],
-                     (row, x * Z + z_peer(2 * sign)))
+    def pass_on(which, buffer):
+        drain(buffer.at[pl.ds(0, 2)], near_recv.at[which + 2])
+        for sign in (1, -1):
+            block = z_peer(-2 * sign)
+            part = pl.ds(0 if sign == 1 else bc // 2, bc // 2)
+            send(buffer.at[block], buffer.at[block], near_send.at[0], near_recv.at[which],
+                 (row, x * Z + z_peer(sign)))
+            send(buffer.at[block, part, :], buffer.at[block, part, :], near_send.at[0], near_recv.at[which],
+                 (row, x * Z + z_peer(2 * sign)))
 
     half = Z // 2
 
@@ -218,6 +217,7 @@
     source = lax.broadcasted_iota(jnp.int32, (nrhs, width), 0)
     lane = lax.broadcasted_iota(jnp.int32, (nrhs, width), 1)
     rhs_second = contract(rhs[1], chosen(source, lane, z))
+    pass_on(0, cross_all)
     drain(first_landed, first_recv.at[0])
     total = first_own[row]
     for slot in range(R - 1):
@@ -238,9 +238,9 @@
                 @pl.when(block == z)
                 def _():
                     pltpu.make_async_copy(first_piece.at[side], target, first_recv.at[1]).start()
-    pass_on()
+    pass_on(1, diag_all)
     ring_pass(1)
-    drain(cross_all.at[pl.ds(0, Z - 3)], near_recv.at[1])
+    drain(cross_all.at[pl.ds(0, Z - 3)], near_recv.at[0])
     cross_turned[...] = cross_all[...].reshape(Z * bc, br).T
     drain(panels.at[0], first_recv.at[1])
 
@@ -253,7 +253,7 @@
     for peer in row_peers:
         send(first_piece, first_rows.at[row], first_send.at[2], first_recv.at[2], (peer, col))
     ring_pass(2, (0,))
-    drain(diag_all.at[pl.ds(0, Z - 3)], near_recv.at[2])
+    drain(diag_all.at[pl.ds(0, Z - 3)], near_recv.at[1])
     drain(cross_landed, last_recv.at[0])
     for d in range(X - 1):
         crossed = crossed + cross_landed[d].astype(F32)
@@ -359,7 +359,7 @@
                 pltpu.VMEM((R, 2, slab, width), BF16),
                 pltpu.SemaphoreType.DMA((6,)),
                 pltpu.SemaphoreType.DMA((1,)),
-                pltpu.SemaphoreType.DMA((3,)),
+                pltpu.SemaphoreType.DMA((4,)),
                 pltpu.SemaphoreType.DMA((2, 2, Z // 2)),
                 pltpu.SemaphoreType.DMA((2, 2, Z // 2)),
                 pltpu.SemaphoreType.DMA((2,)),

time: 54.8 us -> 54.9 us (level)
  no operation moved by 1% of the time
where the time goes in v6:
time: 54.9 us; the launch traced here: 54.8 us
  Pallas kernels  52.8 us (96%)
  local copies, waits for them, and re-layouts  1.36 us (2%)
  between operations  0.64 us (1%)
    pallas_call x1, Pallas kernels, per_device(): pl.pallas_call(functools.partial(kernel, R, X, Z), out_shape=(pltpu.VMEM(...  52.8 us
    unnamed x2, local copies, waits for them, and re-layouts  1.36 us

profile of v6, /device:TPU:1, one launch (start us, length us, event | category | flops | bytes accessed | tf_op | source)
XLA Modules:
  0.0 54.8 jit_solution(4076171417954162617)
XLA Ops:
  0.6 52.8 %shard_map.68 = (bf16[2,64,1024]{2,1,0:T(8,128)(2,1)S(1)}, f32[32,1024]{1,0:T(8,128)S(1)}) custom-call(bf16[2,128,1024]{2,1,0:T(8,128)(2,1)} %rhs_hbm.1, bf16[2,64,128]{2,1,0:T(8,128)(2,1)} %diag_hbm.1, bf16[64,128]{1,0:T(8,128)(2,1)} %bitcast.7, bf16[2,64,1024]{2,1,0:T(8,128)(2,1)} %bitcast.5, f32[32,1024]{1,0:T(8,128)} %bitcast.6), custom_call_target="tpu_custom_call" | custom-call | tf_op jit(solution)/shard_map/pallas_call | solution.py:329
  53.4 0.7 %copy.9 = bf16[2,64,1024]{2,1,0:T(8,128)(2,1)} copy(bf16[2,64,1024]{2,1,0:T(8,128)(2,1)S(1)} %get-tuple-element.6) | data formatting | bytes 524288
  54.1 0.7 %copy.10 = f32[1024,32]{0,1:T(8,128)} copy(f32[1024,32]{0,1:T(8,128)S(1)} %bitcast.4) | data formatting | bytes 262144

commit v7 on v5

--- a/solution.py
+++ b/solution.py
@@ -118,14 +118,15 @@
 
     pl.semaphore_wait(barrier, (R - 1) + (X - 1) + (Z - 1) + (2 - at_home) * R)
 
-    for slot, peer in enumerate(row_peers):
-        send(first_sent.at[peer], first_landed.at[slot], first_send.at[0], first_recv.at[0], (peer, col))
     for load in loads[2:]:
         load.wait()
     for d in (2, -2, 1, -1):
         for which, buffer in enumerate((cross_all, diag_all)):
             send(buffer.at[z], buffer.at[z], near_send.at[0], near_recv.at[0 if abs(d) == 2 else 1 + which],
                  (row, x * Z + z_peer(d)))
+
+    for slot, peer in enumerate(row_peers):
+        send(first_sent.at[peer], first_landed.at[slot], first_send.at[0], first_recv.at[0], (peer, col))
 
     def pass_on():
         drain(cross_all.at[pl.ds(0, 4)], near_recv.at[0])

time: 54.8 us -> 54.8 us (level)
  no operation moved by 1% of the time
where the time goes in v7:
time: 54.8 us; the launch traced here: 54.7 us
  Pallas kernels  52.7 us (96%)
  local copies, waits for them, and re-layouts  1.36 us (2%)
  between operations  0.64 us (1%)
    pallas_call x1, Pallas kernels, per_device(): pl.pallas_call(functools.partial(kernel, R, X, Z), out_shape=(pltpu.VMEM(...  52.7 us
    unnamed x2, local copies, waits for them, and re-layouts  1.36 us

profile of v7, /device:TPU:1, one launch (start us, length us, event | category | flops | bytes accessed | tf_op | source)
XLA Modules:
  0.0 54.7 jit_solution(10731602781630884689)
XLA Ops:
  0.6 52.7 %shard_map.68 = (bf16[2,64,1024]{2,1,0:T(8,128)(2,1)S(1)}, f32[32,1024]{1,0:T(8,128)S(1)}) custom-call(bf16[2,128,1024]{2,1,0:T(8,128)(2,1)} %rhs_hbm.1, bf16[2,64,128]{2,1,0:T(8,128)(2,1)} %diag_hbm.1, bf16[64,128]{1,0:T(8,128)(2,1)} %bitcast.7, bf16[2,64,1024]{2,1,0:T(8,128)(2,1)} %bitcast.5, f32[32,1024]{1,0:T(8,128)} %bitcast.6), custom_call_target="tpu_custom_call" | custom-call | tf_op jit(solution)/shard_map/pallas_call | solution.py:330
  53.3 0.7 %copy.9 = bf16[2,64,1024]{2,1,0:T(8,128)(2,1)} copy(bf16[2,64,1024]{2,1,0:T(8,128)(2,1)S(1)} %get-tuple-element.6) | data formatting | bytes 524288
  54.0 0.7 %copy.10 = f32[1024,32]{0,1:T(8,128)} copy(f32[1024,32]{0,1:T(8,128)S(1)} %bitcast.4) | data formatting | bytes 262144
